TPU v7x, 512 devices: a whole 4x4x16 slice. The times are simulated.
512 devices in a mesh: queue: 64 (over z_lo, x, core), head: 8 (over y, z_hi).
Axes of the slice: x: 4, y: 4, z: 16 (z_hi: 2, z_lo: 8; z = z_hi * 8 + z_lo), core: 2. Of those that a mesh axis runs over, the one named last changes fastest.
Arguments:
- residual: bfloat16 [32768, 5120], P('queue', 'head'), may hold values from -3 to 3
- queries: bfloat16 [32768, 5120], P('queue', 'head'), may hold values from -1000 to 1000
- keys: bfloat16 [32768, 5120], P('queue', 'head'), may hold values from -4 to 4
- values: bfloat16 [32768, 5120], P('queue', 'head'), may hold values from -6 to 6
- out_weight: bfloat16 [5120, 5120], P('queue', 'head'), may hold values from -0.078125 to 0.078125
- gate_table: float32 [64, 5120], P(None, 'head'), may hold values from 0.5 to 2
- levels: int32 [64], P('queue'), may hold values from 0 to 63, each once
Outputs:
- mixed: bfloat16 [32768, 5120], P('queue', 'head')
All inputs are finite; a program needn't handle non-finite values.
Results may differ from a plain program's by a relative error of at most 0.0034.
Values may be sent and summed in bfloat16 or wider, within the bound.
A program may use at most 64 MiB of HBM per device.

v0:
```python
import math

import jax
import jax.numpy as jnp
from jax import lax
from jax.sharding import PartitionSpec as P

HD = 128


def passed_along(value, axis, steps):
    count = lax.axis_size(axis)
    leading, last = (max(0, -steps), min(count, count - steps))
    return lax.ppermute(value, axis, [(source, source + steps) for source in range(leading, last)])


def head_attention(query_part, key_part, value_part, prior_key, prior_value, first_group):
    score_scale = 1.0 / math.sqrt(query_part.shape[1])
    all_keys = jnp.concatenate([prior_key, key_part], axis=0)
    all_values = jnp.concatenate([prior_value, value_part], axis=0)
    scores = (
        jnp.einsum("qd,kd->qk", query_part, all_keys, preferred_element_type=jnp.float32)
        * score_scale
    )
    column = jnp.arange(all_keys.shape[0], dtype=jnp.int32)
    blocked = first_group & (column < prior_key.shape[0])
    scores = jnp.where(blocked[None, :], -jnp.inf, scores)
    row_max = jnp.max(scores, axis=1, keepdims=True)
    weights = jnp.exp(scores - row_max)
    totals = jnp.sum(weights, axis=1, keepdims=True)
    summed = jnp.dot(weights.astype(jnp.bfloat16), all_values, preferred_element_type=jnp.float32)
    return (summed / totals).astype(jnp.bfloat16)


def shards(residual, queries, keys, values, out_weight, gate_table, levels):
    head_width = HD
    head_count = queries.shape[1] // head_width
    first_group = lax.axis_index("queue") == 0
    prior_keys, prior_values = passed_along((keys, values), "queue", 1)
    outputs = []
    for head_index in range(head_count):
        lower = head_index * head_width
        upper = lower + head_width
        outputs.append(
            head_attention(
                queries[:, lower:upper],
                keys[:, lower:upper],
                values[:, lower:upper],
                prior_keys[:, lower:upper],
                prior_values[:, lower:upper],
                first_group,
            )
        )
    attended = jnp.concatenate(outputs, axis=1)
    gathered = lax.all_gather(attended, "head", axis=1, tiled=True)
    projected = jnp.dot(
        gathered,
        lax.all_gather(out_weight, "queue", axis=0, tiled=True),
        preferred_element_type=jnp.float32,
    )
    level_ids = jnp.arange(gate_table.shape[0], dtype=jnp.int32)
    gate_row = jnp.sum(jnp.where((level_ids == levels[0])[:, None], gate_table, 0.0), axis=0)
    return (residual.astype(jnp.float32) + gate_row[None, :] * projected).astype(jnp.bfloat16)


def solution(mesh):
    placed = (
        P("queue", "head"),
        P("queue", "head"),
        P("queue", "head"),
        P("queue", "head"),
        P("queue", "head"),
        P(None, "head"),
        P("queue"),
    )
    return jax.shard_map(
        shards, mesh=mesh, in_specs=placed, out_specs=P("queue", "head"), check_vma=False
    )
```

profile of v0, /device:TPU:1, one launch (start us, length us, event | category | flops | bytes accessed | tf_op | source)
XLA Modules:
  0.0 382.6 jit_solution(14880609178228281972)
XLA Ops:
  6.5 0.0 copy-start.1
  6.5 0.0 all-gather.3.cloned.1.call-start
  6.5 4.6 %collective-permute-start = (bf16[512,640]{1,0:T(8,128)(2,1)}, bf16[512,640]{1,0:T(8,128)(2,1)S(1)}, u32[]{:S(2)}, u32[]{:S(2)}) collective-permute-start(bf16[512,640]{1,0:T(8,128)(2,1)} %param.9), channel_id=1, source_target_pairs={{0,8},{8,16},{16,24},{24,32},{32,40},{40,48},{48,56},{56,64},{64,7... | collective-permute-start | bytes 1966088 | tf_op jit(solution)/shard_map/ppermute | solution.py:14
  11.2 1.9 collective-permute-start.1
  13.1 1.2 fusion.111
  14.4 1.2 fusion.109
  15.6 3.4 collective-permute-done
  19.0 0.1 fusion.110
  19.1 0.0 copy-done.1
  19.1 0.4 fusion.47
  19.6 0.4 fusion.61
  20.0 0.6 fusion.4
  20.6 0.4 fusion.68
  21.1 1.8 fusion.13
  22.9 3.2 collective-permute-done.1
  26.0 0.1 fusion.108
  26.1 0.8 fusion.18
  27.0 1.8 fusion.11
  28.8 0.9 fusion.20
  29.7 0.9 fusion.22
  30.5 0.9 fusion.24
  31.4 0.0 copy-start.2
  31.4 0.0 copy-start.3
  31.4 0.9 fusion.26
  32.3 0.0 copy-start
  32.3 0.8 copy-done
  33.2 0.0 all-gather.3.cloned.1.call-update
  33.2 0.2 all-gather.5.cloned.1.call-start
  33.4 0.5 all-gather.5.cloned.1.call-update
  34.6 0.0 copy-done.2
  34.6 0.1 select_reduce_fusion
  34.7 198.4 %all-gather.3.cloned.1.call-done = bf16[512,5120]{1,0:T(8,128)(2,1)} async-done(((bf16[512,640]{1,0:T(8,128)(2,1)}), bf16[512,5120]{1,0:T(8,128)(2,1)}) %all-gather.3.cloned.1.call-update) | async-done | bytes 5242896 | tf_op jit(solution)/shard_map/all_gather | solution.py:55
  233.1 133.2 %all-gather.5.cloned.1.call-done = bf16[5120,640]{1,0:T(8,128)(2,1)} async-done(((bf16[80,640]{1,0:T(8,128)(2,1)}), bf16[5120,640]{1,0:T(8,128)(2,1)}) %all-gather.5.cloned.1.call-update) | async-done | bytes 6553616 | tf_op jit(solution)/shard_map/all_gather | solution.py:58
  366.3 0.0 copy-done.3
  366.3 9.5 %fusion.16 = bf16[512,640]{1,0:T(8,128)(2,1)} fusion(bf16[512,5120]{1,0:T(8,128)(2,1)} %all-gather.3.cloned.1.call-done, bf16[5120,640]{1,0:T(8,128)(2,1)} %all-gather.5.cloned.1.call-done, bf16[512,640]{1,0:T(8,128)(2,1)S(1)} %copy-done.3, f32[640]{0:T(1024)S(1)} %select_reduce_fusion), kind=kOutput, calls=%fused_computation.27 | convolution fusion | flops 3356753920 | bytes 13109760 | tf_op jit(solution)/shard_map/dot_general | solution.py:56
  (2 shorter events, 0.0 us)
Async XLA Ops:
  6.5 12.6 %copy-start.1 = (bf16[512,640]{1,0:T(8,128)(2,1)S(1)}, bf16[512,640]{1,0:T(8,128)(2,1)}, u32[]{:S(2)}) copy-start(bf16[512,640]{1,0:T(8,128)(2,1)} %param.8) | copy-start | bytes 1966084
  6.5 226.6 %all-gather.3.cloned.1.call-start = ((), (), s32[]{:S(2)}) async-start(), calls=%async_computation | async-start | bytes 5898240 | tf_op jit(solution)/shard_map/all_gather | solution.py:55
  6.5 12.5 %collective-permute-start = (bf16[512,640]{1,0:T(8,128)(2,1)}, bf16[512,640]{1,0:T(8,128)(2,1)S(1)}, u32[]{:S(2)}, u32[]{:S(2)}) collective-permute-start(bf16[512,640]{1,0:T(8,128)(2,1)} %param.9), channel_id=1, source_target_pairs={{0,8},{8,16},{16,24},{24,32},{32,40},{40,48},{48,56},{56,64},{64,7... | collective-permute-start | bytes 1966088 | tf_op jit(solution)/shard_map/ppermute | solution.py:14
  11.2 14.8 %collective-permute-start.1 = (bf16[512,640]{1,0:T(8,128)(2,1)}, bf16[512,640]{1,0:T(8,128)(2,1)S(1)}, u32[]{:S(2)}, u32[]{:S(2)}) collective-permute-start(bf16[512,640]{1,0:T(8,128)(2,1)} %param.10), channel_id=1, source_target_pairs={{0,8},{8,16},{16,24},{24,32},{32,40},{40,48},{48,56},{56,64},{64,7... | collective-permute-start | bytes 1966088 | tf_op jit(solution)/shard_map/ppermute | solution.py:14
  31.4 3.2 copy-start.2
  31.4 334.9 %copy-start.3 = (bf16[512,640]{1,0:T(8,128)(2,1)S(1)}, bf16[512,640]{1,0:T(8,128)(2,1)}, u32[]{:S(2)}) copy-start(bf16[512,640]{1,0:T(8,128)(2,1)} %param.7) | copy-start | bytes 1966084
  32.3 0.8 copy-start
  33.2 333.1 %all-gather.5.cloned.1.call-start = ((), (), s32[]{:S(2)}) async-start(), calls=%async_computation.1 | async-start | bytes 6656000 | tf_op jit(solution)/shard_map/all_gather | solution.py:58
Sparse Core Ops, SparseCore 0:
  33.3 199.7 all-gather.2
  235.2 131.0 all-gather.4
where the time goes:
time: 383 us
  waiting for transfers between devices  339 us (89%)
  matrix products  17.6 us (5%)
  between operations  14.2 us (4%)
  starting transfers between devices  6.78 us (2%)
    all_gather x1, waiting for transfers between devices, shards(): gathered = lax.all_gather(attended, 'head', axis=1, tiled=True)  198 us
    all_gather x1, waiting for transfers between devices, shards(): lax.all_gather(out_weight, 'queue', axis=0, tiled=True)  133 us
    dot_general x1, matrix products, shards(): jnp.dot(gathered, lax.all_gather(out_weight, 'queue', axis=0, tiled=True)...  9.48 us
  transfers between devices with their start and end apart: 4, of which 4 were waited for; matrix products, arithmetic and copies ran while one was open for 2% of the time, Pallas kernels for 0%

commit v1 on v0

v1 whole, which is shorter than its diff:
```python
import functools
import math

import jax
import jax.numpy as jnp
from jax import lax
from jax.experimental import pallas as pl
from jax.experimental.pallas import tpu as pltpu
from jax.sharding import PartitionSpec as P

HD = 128
XS, YS, CORES, ZH = 4, 4, 2, 2
MESH = pl.DeviceIdType.MESH
ROWS = 256


def kernel(
    zl_count,
    res_hbm, q_hbm, k_hbm, v_hbm, w_hbm, gate_ref, level_ref,
    out_hbm,
    q_ref, k_ref, v_ref, res_ref, out_ref, pk_ref, pv_ref, w_ref, a_ref, acc_ref,
    load_sem, store_sem,
    kv_send, kv_recv, wz_up, wz_down, wz_recv, wx_send, wx_recv, ws_send, ws_recv,
    az_send, az_recv, ay_send, ay_own, ay_far,
):
    tokens, width = q_ref.shape
    heads = width // HD
    parts = tokens // ROWS
    pieces = heads * parts
    depth = w_hbm.shape[0]
    queue_count = zl_count * XS * CORES

    queue = lax.axis_index("queue")
    head = lax.axis_index("head")
    core = lax.rem(queue, CORES)
    x = lax.rem(queue // CORES, XS)
    zl = queue // (CORES * XS)
    y = head // ZH
    zh = lax.rem(head, ZH)

    sibling = (queue + 1 - 2 * core, head)
    partner = (queue, head + 1 - 2 * zh)
    far = head + 1 - 2 * zh

    def x_peer(k):
        return (queue + CORES * (lax.rem(x + k, XS) - x), head)

    def y_peer(k):
        return (queue, head + ZH * (lax.rem(y + k, YS) - y))

    up, down = (queue + CORES * XS, head), (queue - CORES * XS, head)
    after, before = (queue + 1, head), (queue - 1, head)
    has_up, has_down = zl < zl_count - 1, zl > 0
    has_after, has_before = queue < queue_count - 1, queue > 0

    def remote(src, dst, send, recv, device):
        return pltpu.make_async_remote_copy(
            src_ref=src, dst_ref=dst, send_sem=send, recv_sem=recv, device_id=device, device_id_type=MESH
        )

    def landed(ref, sem):
        pltpu.make_async_copy(ref, ref, sem).wait()

    loads = [
        pltpu.make_async_copy(src, dst, load_sem.at[i])
        for i, (src, dst) in enumerate(((q_hbm, q_ref), (k_hbm, k_ref), (v_hbm, v_ref), (res_hbm, res_ref)))
    ]
    for load in loads:
        load.start()
    block = pl.multiple_of(queue * depth, 16)
    own_w = pltpu.make_async_copy(w_hbm, w_ref.at[pl.ds(block, depth)], load_sem.at[4])
    own_w.start()

    barrier = pltpu.get_barrier_semaphore()
    greet = [sibling, partner] + [x_peer(k) for k in (1, 2, 3)] + [y_peer(k) for k in (1, 2, 3)]
    for device in greet:
        pl.semaphore_signal(barrier, inc=1, device_id=device, device_id_type=MESH)
    for there, device in ((has_up, up), (has_down, down), (has_after, after), (has_before, before)):
        @pl.when(there)
        def _():
            pl.semaphore_signal(barrier, inc=1, device_id=device, device_id_type=MESH)
    edges = sum(there.astype(jnp.int32) for there in (has_up, has_down, has_after, has_before))
    pl.semaphore_wait(barrier, len(greet) + edges)

    @pl.when(has_after)
    def _():
        for h in range(heads):
            columns = pl.ds(h * HD, HD)
            remote(k_hbm.at[:, columns], pk_ref.at[h], kv_send, kv_recv.at[0, h], after).start()
            remote(v_hbm.at[:, columns], pv_ref.at[h], kv_send, kv_recv.at[1, h], after).start()

    def w_rows(zl_from, x_from, core_from):
        index = (zl_from * XS + x_from) * CORES + core_from
        return w_ref.at[pl.ds(pl.multiple_of(index * depth, 16), depth)]

    def w_up(zl_from, src):
        remote(src, w_rows(zl_from, x, core), wz_up.at[zl_from], wz_recv.at[zl_from], up).start()

    def w_down(zl_from, src):
        remote(src, w_rows(zl_from, x, core), wz_down.at[zl_from], wz_recv.at[zl_from], down).start()

    def w_across(zl_from, src):
        dst = w_rows(zl_from, x, core)
        for k in (1, 3, 2):
            remote(src, dst, wx_send, wx_recv.at[k - 1], x_peer(k)).start()
        remote(src, dst, ws_send, ws_recv, sibling).start()

    @pl.when(has_up)
    def _():
        w_up(zl, w_hbm)

    @pl.when(has_down)
    def _():
        w_down(zl, w_hbm)

    def w_step(t):
        low, high = zl - t, zl + t

        @pl.when(low >= 0)
        def _():
            rows = w_rows(low, x, core)
            landed(rows, wz_recv.at[low])

            @pl.when(has_up)
            def _():
                w_up(low, rows)

            w_across(low, rows)

        @pl.when(high < zl_count)
        def _():
            rows = w_rows(high, x, core)
            landed(rows, wz_recv.at[high])

            @pl.when(has_down)
            def _():
                w_down(high, rows)

            w_across(high, rows)

    @pl.when(jnp.logical_not(has_before))
    def _():
        pk_ref[...] = jnp.zeros_like(pk_ref)
        pv_ref[...] = jnp.zeros_like(pv_ref)

    levels = lax.broadcasted_iota(jnp.int32, gate_ref.shape, 0)
    gate_row = jnp.sum(jnp.where(levels == level_ref[0], gate_ref[...], 0.0), axis=0, keepdims=True)
    blocked = jnp.where(has_before, 0.0, -1e30).astype(jnp.float32)

    for load in loads:
        load.wait()
    own_w.wait()

    def piece(source, p):
        h, part = p // parts, p % parts
        return a_ref.at[source, h, pl.ds(part * ROWS, ROWS)]

    scale = math.log2(math.e) / math.sqrt(HD)
    contract_last = (((1,), (1,)), ((), ()))
    for h in range(heads):
        columns = pl.ds(h * HD, HD)

        @pl.when(has_before)
        def _():
            landed(pk_ref.at[h], kv_recv.at[0, h])
            landed(pv_ref.at[h], kv_recv.at[1, h])

        for part in range(parts):
            rows = pl.ds(part * ROWS, ROWS)
            queries = q_ref[rows, columns]
            own = lax.dot_general(queries, k_ref[:, columns], contract_last, preferred_element_type=jnp.float32) * scale
            prior = lax.dot_general(queries, pk_ref[h], contract_last, preferred_element_type=jnp.float32) * scale + blocked
            row_max = jnp.maximum(jnp.max(own, axis=1, keepdims=True), jnp.max(prior, axis=1, keepdims=True))
            own = jnp.exp2(own - row_max)
            prior = jnp.exp2(prior - row_max)
            totals = jnp.sum(own, axis=1, keepdims=True) + jnp.sum(prior, axis=1, keepdims=True)
            summed = jnp.dot(own.astype(jnp.bfloat16), v_ref[:, columns], preferred_element_type=jnp.float32)
            summed += jnp.dot(prior.astype(jnp.bfloat16), pv_ref[h], preferred_element_type=jnp.float32)
            a_ref[head, h, rows] = (summed / totals).astype(jnp.bfloat16)
            p = h * parts + part
            remote(piece(head, p), piece(head, p), az_send, az_recv.at[p], partner).start()
            for k in (1, 3, 2):
                remote(piece(head, p), piece(head, p), ay_send, ay_own.at[k - 1], y_peer(k)).start()
        if h == 0:
            w_across(zl, w_hbm)
        else:
            w_step(h)
    for t in range(heads, zl_count):
        w_step(t)

    def w_pass(k):
        landed(w_ref.at[pl.ds(0, zl_count * depth)], wx_recv.at[k - 1])
        for zl_from in range(zl_count):
            rows = w_rows(zl_from, lax.rem(x + XS - k, XS), core)
            remote(rows, rows, ws_send, ws_recv, sibling).start()

    def project(source, first_head, last_head, part, first=False):
        rows = pl.ds(part * ROWS, ROWS)
        deep = (last_head - first_head) * HD
        left = jnp.concatenate([a_ref[source, h, rows] for h in range(first_head, last_head)], axis=1)
        start = pl.multiple_of(source * width + first_head * HD, HD)
        term = jnp.dot(left, w_ref[pl.ds(start, deep)], preferred_element_type=jnp.float32)
        if first:
            acc_ref[rows] = term
        else:
            acc_ref[rows] += term

    def far_landed(k, p):
        landed(piece(far, p), ay_far.at[k - 1, p])

    def far_of(k):
        return ZH * lax.rem(y + YS - k, YS) + 1 - zh

    early = (heads - 1) * parts
    for p in range(pieces):
        landed(piece(far, p), az_recv.at[p])
        for k in (1, 3, 2):
            remote(piece(far, p), piece(far, p), ay_send, ay_far.at[k - 1, p], y_peer(k)).start()
        if p in (pieces - 5, pieces - 4, pieces - 3):
            w_pass((1, 3, 2)[p - (pieces - 5)])
        if p == pieces - 2:
            landed(w_ref.at[pl.ds(0, queue_count * depth // 2)], ws_recv)
            for part in range(parts):
                project(head, 0, heads, part, first=True)
            for k in (1, 2, 3):
                landed(a_ref.at[0], ay_own.at[k - 1])
                for part in range(parts):
                    project(ZH * lax.rem(y + YS - k, YS) + zh, 0, heads, part)
            for part in range(parts):
                project(far, 0, heads - 1, part)
            for k in (1, 3, 2):
                for e in range(early):
                    far_landed(k, e)
                for part in range(parts):
                    project(far_of(k), 0, heads - 1, part)
    stores = []
    for part in range(parts):
        project(far, heads - 1, heads, part)
        for k in (1, 3, 2):
            far_landed(k, early + part)
            project(far_of(k), heads - 1, heads, part)
        rows = pl.ds(part * ROWS, ROWS)
        out_ref[rows] = (res_ref[rows].astype(jnp.float32) + gate_row * acc_ref[rows]).astype(jnp.bfloat16)
        store = pltpu.make_async_copy(out_ref.at[rows], out_hbm.at[rows], store_sem.at[part])
        store.start()
        stores.append(store)

    @pl.when(has_after)
    def _():
        landed(w_ref.at[pl.ds(0, 2 * tokens)], kv_send)

    for t in range(zl_count):
        @pl.when(jnp.logical_and(has_up, zl >= t))
        def _():
            landed(w_rows(t, x, core), wz_up.at[t])

        @pl.when(jnp.logical_and(has_down, zl <= t))
        def _():
            landed(w_rows(t, x, core), wz_down.at[t])

    landed(w_ref.at[pl.ds(0, 3 * zl_count * depth)], wx_send)
    landed(w_ref.at[pl.ds(0, XS * zl_count * depth)], ws_send)
    landed(a_ref.at[0], az_send)
    landed(a_ref.at[pl.ds(0, 6)], ay_send)
    for store in stores:
        store.wait()


def shards(residual, queries, keys, values, out_weight, gate_table, levels):
    tokens, width = queries.shape
    heads = width // HD
    pieces = heads * (tokens // ROWS)
    sources = lax.axis_size("head")
    queue_count = lax.axis_size("queue")
    zl_count = queue_count // (XS * CORES)
    whole = out_weight.shape[0] * queue_count
    bf16 = jnp.bfloat16
    dma = pltpu.SemaphoreType.DMA
    anywhere = pl.BlockSpec(memory_space=pl.ANY)
    return pl.pallas_call(
        functools.partial(kernel, zl_count),
        out_shape=jax.ShapeDtypeStruct(residual.shape, bf16),
        in_specs=[anywhere] * 5 + [pl.BlockSpec(memory_space=pltpu.VMEM), pl.BlockSpec(memory_space=pltpu.SMEM)],
        out_specs=anywhere,
        scratch_shapes=[
            pltpu.VMEM((tokens, width), bf16),
            pltpu.VMEM((tokens, width), bf16),
            pltpu.VMEM((tokens, width), bf16),
            pltpu.VMEM((tokens, width), bf16),
            pltpu.VMEM((tokens, width), bf16),
            pltpu.VMEM((heads, tokens, HD), bf16),
            pltpu.VMEM((heads, tokens, HD), bf16),
            pltpu.VMEM((whole, width), bf16),
            pltpu.VMEM((sources, heads, tokens, HD), bf16),
            pltpu.VMEM((tokens, width), jnp.float32),
            dma((5,)),
            dma((tokens // ROWS,)),
            dma,
            dma((2, heads)),
            dma((zl_count,)),
            dma((zl_count,)),
            dma((zl_count,)),
            dma,
            dma((3,)),
            dma,
            dma,
            dma,
            dma((pieces,)),
            dma,
            dma((3,)),
            dma((3, pieces)),
        ],
        compiler_params=pltpu.CompilerParams(
            collective_id=0, has_side_effects=True, vmem_limit_bytes=56 * 2**20
        ),
    )(residual, queries, keys, values, out_weight, gate_table, levels)


def solution(mesh):
    placed = (
        P("queue", "head"),
        P("queue", "head"),
        P("queue", "head"),
        P("queue", "head"),
        P("queue", "head"),
        P(None, "head"),
        P("queue"),
    )
    return jax.shard_map(
        shards, mesh=mesh, in_specs=placed, out_specs=P("queue", "head"), check_vma=False
    )
```

time: 383 us -> 133 us (0.35)
  waiting for transfers between devices: 339 us -> 0 us
  Pallas kernels: 0 us -> 128 us
  matrix products: 17.6 us -> 0 us
  between operations: 14.2 us -> 0.66 us
  starting transfers between devices: 6.78 us -> 0 us
    all_gather x2 -> x0, waiting for transfers between devices: 332 us -> none  [the longest x1 198 us: shards(): gathered = lax.all_gather(attended, 'head', axis=1, tiled=True)]
    pallas_call x0 -> x1, Pallas kernels: none -> 128 us  [shards(): pl.pallas_call(functools.partial(kernel, zl_count), out_shape=jax.ShapeDt...]
    dot_general x11 -> x0, matrix products: 17.6 us -> none  [the longest x1 9.48 us: shards(): jnp.dot(gathered, lax.all_gather(out_weight, 'queue', axis=0, tiled=True)...]
    ppermute x2 -> x0, waiting for transfers between devices: 6.58 us -> none  [passed_along(): lax.ppermute(value, axis, [(source, source + steps) for source in range(l...]
    ppermute x2 -> x0, starting transfers between devices: 6.55 us -> none  [passed_along(): lax.ppermute(value, axis, [(source, source + steps) for source in range(l...]
  transfers between devices with their start and end apart: 4 -> 0, of which waited for: 4 -> 0; matrix products, arithmetic and copies ran while one was open for 2% -> 0% of each run, Pallas kernels for 0% -> 0%
where the time goes in v1:
time: 133 us; the launch traced here: 130 us
  Pallas kernels  128 us (96%)
  local copies, waits for them, and re-layouts  1.98 us (1%)
    pallas_call x1, Pallas kernels, shards(): pl.pallas_call(functools.partial(kernel, zl_count), out_shape=jax.ShapeDt...  128 us

profile of v1, /device:TPU:1, one launch (start us, length us, event | category | flops | bytes accessed | tf_op | source)
XLA Modules:
  0.0 130.4 jit_solution(14779986817381610840)
XLA Ops:
  0.7 127.8 %shard_map.73 = bf16[512,640]{1,0:T(8,128)(2,1)} custom-call(bf16[512,640]{1,0:T(8,128)(2,1)} %res_hbm.1, bf16[512,640]{1,0:T(8,128)(2,1)} %q_hbm.1, bf16[512,640]{1,0:T(8,128)(2,1)} %k_hbm.1, bf16[512,640]{1,0:T(8,128)(2,1)} %v_hbm.1, bf16[80,640]{1,0:T(8,128)(2,1)} %w_hbm.1, f32[64,640]{1,0:T(8,128)} %gate_ref.1, s32[1]{0:T(128)S(6)} %copy.9.level_ref), custom_call_target="tpu_custom_call" | custom-call | tf_op jit(solution)/shard_map/pallas_call | solution.py:280
  128.4 2.0 %copy.10 = bf16[512,640]{1,0:T(8,128)(2,1)} copy(bf16[512,640]{1,0:T(8,128)(2,1)} %shard_map.73) | data formatting | bytes 1310720

commit v2 on v1

v2 whole, which is shorter than its diff:
```python
import functools
import math

import jax
import jax.numpy as jnp
from jax import lax
from jax.experimental import pallas as pl
from jax.experimental.pallas import tpu as pltpu
from jax.sharding import PartitionSpec as P

HD = 128
XS, YS, CORES, ZH = 4, 4, 2, 2
MESH = pl.DeviceIdType.MESH
ROWS = 256
HOPS = 8
STEPS = (
    "w0 w1 x30 a0", "r0 z00 r1 a1", "r2 z10 a2 w2", "r3 x31 z01 Y0", "a3 r4 z11 Y1", "x20 z20 z30 Y2", "a4 w3 x32 a5", "z02 z12 Y3 x21", "a6 z21 z31 a7", "w4 x33 Y4 Y5", "x10 a8 z03 z13", "z22 z32 Y6 x22", "x11 a9 x34 Y7", "w5 x12 z04 z14", "Y8 x23 x13 z23", "z33 Y9 x24 x14", "w6 x35 x15 z05", "z15 z24 z34 x36", "x16 w7 z40 z50", "x25 z06 z16 z25", "z35 x26 x17 z41", "z51 x37 z07 z17", "z26 z36 z42 z52", "x27 f0 f1 z60", "z70 z27 z37 o0", "F0 z43 z53 o1", "F1 z61 z71 o2", "f2 f3 z80 z90", "o3 z44 z54 z62", "z72 F2 z81 z91", "F3 g010 z45 z55", "g011 g013 z63 z73", "g012 z82 z92 z46", "z56 z64 z74 z83", "z93 z47 z57 z65", "z75 z84 z94 f4", "f5 z66 z76 z85", "F4 z95 z67 F5", "z77 z86 z96 f6", "f7 z87 z97 F6", "f8 F7 f9 g230", "g231 g233 F8 g232", "F9",
)


def kernel(
    zl_count,
    res_hbm, q_hbm, k_hbm, v_hbm, w_hbm, gate_ref, level_ref,
    out_hbm,
    q_ref, k_ref, v_ref, res_ref, out_ref, pk_ref, pv_ref, relay_ref, w_ref, a_ref, hop_ref, acc_ref,
    load_sem, store_sem,
    kv_send, kv_recv, relay_send, relay_recv, wz_up, wz_down, wz_recv, wx_send, wx_recv, ws_send, ws_recv,
    hop_send, hop_recv, ay_send, ay_own, ay_far,
):
    tokens, width = q_ref.shape
    heads = width // HD
    parts = tokens // ROWS
    pieces = heads * parts
    depth = w_hbm.shape[0]
    queue_count = zl_count * XS * CORES

    queue = lax.axis_index("queue")
    head = lax.axis_index("head")
    core = lax.rem(queue, CORES)
    x = lax.rem(queue // CORES, XS)
    zl = queue // (CORES * XS)
    y = head // ZH
    zh = lax.rem(head, ZH)

    sibling = (queue + 1 - 2 * core, head)
    far = head + 1 - 2 * zh

    def x_peer(k):
        return (queue + CORES * (lax.rem(x + k, XS) - x), head)

    def y_peer(k):
        return (queue, head + ZH * (lax.rem(y + k, YS) - y))

    def ring_peer(way):
        z = lax.rem(zh * zl_count + zl + way + ZH * zl_count, ZH * zl_count)
        there = z // zl_count
        return (queue + CORES * XS * (lax.rem(z, zl_count) - zl), head + there - zh), y * ZH + 1 - there

    up, down = (queue + CORES * XS, head), (queue - CORES * XS, head)
    after, before = (queue + 1, head), (queue - 1, head)
    has_up, has_down = zl < zl_count - 1, zl > 0
    has_after, has_before = queue < queue_count - 1, queue > 0
    crosses = (core == 1) & (x == XS - 1) & has_up
    by_x = (core == 1) & (x == 0) & has_up
    by_z = (core == 1) & (x == XS - 1) & has_down
    crossed = (core == 0) & (x == 0) & has_down
    over = CORES * XS - 1
    forward, back = (queue + over, head), (queue - over, head)

    def remote(src, dst, send, recv, device):
        return pltpu.make_async_remote_copy(
            src_ref=src, dst_ref=dst, send_sem=send, recv_sem=recv, device_id=device, device_id_type=MESH
        )

    def landed(ref, sem):
        pltpu.make_async_copy(ref, ref, sem).wait()

    loads = [
        pltpu.make_async_copy(src, dst, load_sem.at[i])
        for i, (src, dst) in enumerate(((q_hbm, q_ref), (k_hbm, k_ref), (v_hbm, v_ref), (res_hbm, res_ref)))
    ]
    for load in loads:
        load.start()
    block = pl.multiple_of(queue * depth, 16)
    own_w = pltpu.make_async_copy(w_hbm, w_ref.at[pl.ds(block, depth)], load_sem.at[4])
    own_w.start()

    barrier = pltpu.get_barrier_semaphore()
    greet = [sibling, ring_peer(1)[0], ring_peer(-1)[0]] + [x_peer(k) for k in (1, 3)] + [y_peer(k) for k in (1, 3)]
    for device in greet:
        pl.semaphore_signal(barrier, inc=1, device_id=device, device_id_type=MESH)
    edges = (
        (has_after, after), (has_before, before),
        (by_x | crossed, forward), (by_z | crossed, back),
    )
    for there, device in edges:
        @pl.when(there)
        def _():
            pl.semaphore_signal(barrier, inc=1, device_id=device, device_id_type=MESH)
    pl.semaphore_wait(barrier, len(greet) + sum(there.astype(jnp.int32) for there, _ in edges))

    @pl.when(has_after & jnp.logical_not(crosses))
    def _():
        for h in range(heads):
            columns = pl.ds(h * HD, HD)
            remote(k_hbm.at[:, columns], pk_ref.at[h], kv_send, kv_recv.at[0, h], after).start()
            remote(v_hbm.at[:, columns], pv_ref.at[h], kv_send, kv_recv.at[1, h], after).start()

    @pl.when(crosses)
    def _():
        for h in range(heads):
            columns = pl.ds(h * HD, HD)
            remote(k_hbm.at[:, columns], relay_ref.at[h], kv_send, relay_recv.at[h], x_peer(1)).start()
            remote(v_hbm.at[:, columns], relay_ref.at[h], kv_send, relay_recv.at[h], up).start()

    def pass_on(h):
        @pl.when(by_x)
        def _():
            landed(relay_ref.at[h], relay_recv.at[h])
            remote(relay_ref.at[h], pk_ref.at[h], relay_send, kv_recv.at[0, h], forward).start()

        @pl.when(by_z)
        def _():
            landed(relay_ref.at[h], relay_recv.at[h])
            remote(relay_ref.at[h], pv_ref.at[h], relay_send, kv_recv.at[1, h], back).start()

    def w_rows(zl_from, x_from, core_from):
        index = (zl_from * XS + x_from) * CORES + core_from
        return w_ref.at[pl.ds(pl.multiple_of(index * depth, 16), depth)]

    def w_up(zl_from, src):
        @pl.when(has_up)
        def _():
            remote(src, w_rows(zl_from, x, core), wz_up.at[zl_from], wz_recv.at[zl_from], up).start()

    def w_down(zl_from, src):
        @pl.when(has_down)
        def _():
            remote(src, w_rows(zl_from, x, core), wz_down.at[zl_from], wz_recv.at[zl_from], down).start()

    def w_across(zl_from, src):
        dst = w_rows(zl_from, x, core)
        for k in (1, 3):
            remote(src, dst, wx_send, wx_recv.at[k - 1, zl_from], x_peer(k)).start()
        remote(src, dst, ws_send, ws_recv, sibling).start()

    w_up(zl, w_hbm)
    w_down(zl, w_hbm)

    def w_both(t, work):
        @pl.when(zl >= t)
        def _():
            work(zl - t, w_up)

        if t > 0:
            @pl.when(zl + t < zl_count)
            def _():
                work(zl + t, w_down)

    def w_hop(t):
        def work(zl_from, onward):
            rows = w_rows(zl_from, x, core)
            landed(rows, wz_recv.at[zl_from])
            onward(zl_from, rows)
            w_across(zl_from, rows)

        if t == 0:
            w_across(zl, w_hbm)
        else:
            w_both(t, work)

    def w_pass(k, t):
        def work(zl_from, _):
            rows = w_rows(zl_from, lax.rem(x + XS - k, XS), core)
            landed(rows, wx_recv.at[k - 1, zl_from])
            if k == 3:
                remote(rows, rows, wx_send, wx_recv.at[1, zl_from], x_peer(3)).start()
            remote(rows, rows, ws_send, ws_recv, sibling).start()

        w_both(t, work)

    @pl.when(jnp.logical_not(has_before))
    def _():
        pk_ref[...] = jnp.zeros_like(pk_ref)
        pv_ref[...] = jnp.zeros_like(pv_ref)

    levels = lax.broadcasted_iota(jnp.int32, gate_ref.shape, 0)
    gate_row = jnp.sum(jnp.where(levels == level_ref[0], gate_ref[...], 0.0), axis=0, keepdims=True)
    blocked = jnp.where(has_before, 0.0, -1e30).astype(jnp.float32)

    for load in loads:
        load.wait()
    own_w.wait()

    def piece(source, p):
        h, part = p // parts, p % parts
        return a_ref.at[source, h, pl.ds(part * ROWS, ROWS)]

    def z_hop(p, hop):
        device, last = ring_peer(1 - 2 * (p % 2))
        src = piece(head, p)
        if hop > 0:
            src = hop_ref.at[p, hop - 1]
            landed(src, hop_recv.at[p, hop - 1])
        dst = hop_ref.at[p, hop] if hop < HOPS - 1 else piece(last, p)
        remote(src, dst, hop_send, hop_recv.at[p, hop], device).start()

    def y_send(source, p, arrived):
        for k in (1, 3):
            remote(piece(source, p), piece(source, p), ay_send, arrived.at[k - 1, p], y_peer(k)).start()

    scale = math.log2(math.e) / math.sqrt(HD)
    contract_last = (((1,), (1,)), ((), ()))

    def attend(p):
        h, part = p // parts, p % parts
        columns = pl.ds(h * HD, HD)
        rows = pl.ds(part * ROWS, ROWS)
        if part == 0:
            @pl.when(has_before)
            def _():
                landed(pk_ref.at[h], kv_recv.at[0, h])
                landed(pv_ref.at[h], kv_recv.at[1, h])

        queries = q_ref[rows, columns]
        own = lax.dot_general(queries, k_ref[:, columns], contract_last, preferred_element_type=jnp.float32) * scale
        prior = lax.dot_general(queries, pk_ref[h], contract_last, preferred_element_type=jnp.float32) * scale + blocked
        row_max = jnp.maximum(jnp.max(own, axis=1, keepdims=True), jnp.max(prior, axis=1, keepdims=True))
        own = jnp.exp2(own - row_max)
        prior = jnp.exp2(prior - row_max)
        totals = jnp.sum(own, axis=1, keepdims=True) + jnp.sum(prior, axis=1, keepdims=True)
        summed = jnp.dot(own.astype(jnp.bfloat16), v_ref[:, columns], preferred_element_type=jnp.float32)
        summed += jnp.dot(prior.astype(jnp.bfloat16), pv_ref[h], preferred_element_type=jnp.float32)
        a_ref[head, h, rows] = (summed / totals).astype(jnp.bfloat16)
        y_send(head, p, ay_own)

    def project(source, first_head, last_head, part, first=False):
        rows = pl.ds(part * ROWS, ROWS)
        deep = (last_head - first_head) * HD
        left = jnp.concatenate([a_ref[source, h, rows] for h in range(first_head, last_head)], axis=1)
        start = pl.multiple_of(source * width + first_head * HD, HD)
        term = jnp.dot(left, w_ref[pl.ds(start, deep)], preferred_element_type=jnp.float32)
        if first:
            acc_ref[rows] = term
        else:
            acc_ref[rows] += term

    def source_of(k, side):
        return ZH * lax.rem(y + YS - k, YS) + side

    seen = set()

    def y_landed(k, side, p):
        if k > 0 and (k, side is zh, p) not in seen:
            seen.add((k, side is zh, p))
            landed(piece(source_of(k, side), p), (ay_own if side is zh else ay_far).at[k - 1, p])

    def y_pass(side, p):
        k = 1 if p % 2 == 0 else 3
        y_landed(k, side, p)
        ref = piece(source_of(k, side), p)
        arrived = ay_own if side is zh else ay_far
        remote(ref, ref, ay_send, arrived.at[1, p], y_peer(k)).start()

    def project_source(k, side, first_head, last_head, part, first=False):
        for h in range(first_head, last_head):
            y_landed(k, side, h * parts + part)
        project(source_of(k, side), first_head, last_head, part, first)

    other = 1 - zh
    weights_here = False
    for step in " ".join(STEPS).split():
        kind, numbers = step[0], [int(c) for c in step[1:]]
        if kind == "a":
            attend(*numbers)
        elif kind == "r":
            pass_on(*numbers)
        elif kind == "z":
            z_hop(*numbers)
        elif kind == "f":
            landed(piece(far, numbers[0]), hop_recv.at[numbers[0], HOPS - 1])
            y_send(far, numbers[0], ay_far)
        elif kind == "Y":
            y_pass(zh, *numbers)
        elif kind == "F":
            y_pass(other, *numbers)
        elif kind == "w":
            w_hop(*numbers)
        elif kind == "x":
            w_pass(*numbers)
        else:
            if not weights_here:
                landed(w_ref.at[pl.ds(0, queue_count * depth // 2)], ws_recv)
                weights_here = True
            for part in range(parts):
                if kind == "o":
                    project_source(numbers[0], zh, 0, heads, part, first=numbers[0] == 0)
                else:
                    project_source(numbers[2], other, numbers[0], numbers[1] + 1, part)
    stores = []
    for part in range(parts):
        for k in (0, 1, 3, 2):
            project_source(k, other, heads - 1, heads, part)
        rows = pl.ds(part * ROWS, ROWS)
        out_ref[rows] = (res_ref[rows].astype(jnp.float32) + gate_row * acc_ref[rows]).astype(jnp.bfloat16)
        store = pltpu.make_async_copy(out_ref.at[rows], out_hbm.at[rows], store_sem.at[part])
        store.start()
        stores.append(store)

    @pl.when(by_x | by_z)
    def _():
        landed(relay_ref, relay_send)

    @pl.when(has_after)
    def _():
        landed(w_ref.at[pl.ds(0, 2 * tokens)], kv_send)

    for t in range(zl_count):
        @pl.when(has_up & (zl >= t))
        def _():
            landed(w_rows(t, x, core), wz_up.at[t])

        @pl.when(has_down & (zl <= t))
        def _():
            landed(w_rows(t, x, core), wz_down.at[t])

    landed(w_ref.at[pl.ds(0, 3 * zl_count * depth)], wx_send)
    landed(w_ref.at[pl.ds(0, XS * zl_count * depth)], ws_send)
    landed(a_ref, hop_send)
    landed(a_ref.at[pl.ds(0, 6)], ay_send)
    for store in stores:
        store.wait()


def shards(residual, queries, keys, values, out_weight, gate_table, levels):
    tokens, width = queries.shape
    heads = width // HD
    pieces = heads * (tokens // ROWS)
    sources = lax.axis_size("head")
    queue_count = lax.axis_size("queue")
    zl_count = queue_count // (XS * CORES)
    whole = out_weight.shape[0] * queue_count
    bf16 = jnp.bfloat16
    dma = pltpu.SemaphoreType.DMA
    anywhere = pl.BlockSpec(memory_space=pl.ANY)
    return pl.pallas_call(
        functools.partial(kernel, zl_count),
        out_shape=jax.ShapeDtypeStruct(residual.shape, bf16),
        in_specs=[anywhere] * 5 + [pl.BlockSpec(memory_space=pltpu.VMEM), pl.BlockSpec(memory_space=pltpu.SMEM)],
        out_specs=anywhere,
        scratch_shapes=[
            pltpu.VMEM((tokens, width), bf16),
            pltpu.VMEM((tokens, width), bf16),
            pltpu.VMEM((tokens, width), bf16),
            pltpu.VMEM((tokens, width), bf16),
            pltpu.VMEM((tokens, width), bf16),
            pltpu.VMEM((heads, tokens, HD), bf16),
            pltpu.VMEM((heads, tokens, HD), bf16),
            pltpu.VMEM((heads, tokens, HD), bf16),
            pltpu.VMEM((whole, width), bf16),
            pltpu.VMEM((sources, heads, tokens, HD), bf16),
            pltpu.VMEM((pieces, HOPS - 1, ROWS, HD), bf16),
            pltpu.VMEM((tokens, width), jnp.float32),
            dma((5,)),
            dma((tokens // ROWS,)),
            dma,
            dma((2, heads)),
            dma,
            dma((heads,)),
            dma((zl_count,)),
            dma((zl_count,)),
            dma((zl_count,)),
            dma,
            dma((3, zl_count)),
            dma,
            dma,
            dma,
            dma((pieces, HOPS)),
            dma,
            dma((3, pieces)),
            dma((3, pieces)),
        ],
        compiler_params=pltpu.CompilerParams(
            collective_id=0, has_side_effects=True, vmem_limit_bytes=56 * 2**20
        ),
    )(residual, queries, keys, values, out_weight, gate_table, levels)


def solution(mesh):
    placed = (
        P("queue", "head"),
        P("queue", "head"),
        P("queue", "head"),
        P("queue", "head"),
        P("queue", "head"),
        P(None, "head"),
        P("queue"),
    )
    return jax.shard_map(
        shards, mesh=mesh, in_specs=placed, out_specs=P("queue", "head"), check_vma=False
    )
```

time: 133 us -> 123 us (0.925)
  the two profiles are of different devices: /device:TPU:1 before, /device:TPU:8 now
where the time goes in v2:
time: 123 us; the launch traced here: 122 us
  Pallas kernels  120 us (98%)
  local copies, waits for them, and re-layouts  1.98 us (2%)
    pallas_call x1, Pallas kernels, shards(): pl.pallas_call(functools.partial(kernel, zl_count), out_shape=jax.ShapeDt...  120 us

profile of v2, /device:TPU:8, one launch (start us, length us, event | category | flops | bytes accessed | tf_op | source)
XLA Modules:
  0.0 122.4 jit_solution(2720372231108720538)
XLA Ops:
  0.7 119.8 %shard_map.73 = bf16[512,640]{1,0:T(8,128)(2,1)} custom-call(bf16[512,640]{1,0:T(8,128)(2,1)} %res_hbm.1, bf16[512,640]{1,0:T(8,128)(2,1)} %q_hbm.1, bf16[512,640]{1,0:T(8,128)(2,1)} %k_hbm.1, bf16[512,640]{1,0:T(8,128)(2,1)} %v_hbm.1, bf16[80,640]{1,0:T(8,128)(2,1)} %w_hbm.1, f32[64,640]{1,0:T(8,128)} %gate_ref.1, s32[1]{0:T(128)S(6)} %copy.9.level_ref), custom_call_target="tpu_custom_call" | custom-call | tf_op jit(solution)/shard_map/pallas_call | solution.py:346
  120.4 2.0 %copy.10 = bf16[512,640]{1,0:T(8,128)(2,1)} copy(bf16[512,640]{1,0:T(8,128)(2,1)} %shard_map.73) | data formatting | bytes 1310720

commit v3 on v2

--- a/solution.py
+++ b/solution.py
@@ -12,9 +12,10 @@
 XS, YS, CORES, ZH = 4, 4, 2, 2
 MESH = pl.DeviceIdType.MESH
 ROWS = 256
+KEYS_BY_X = 3
 HOPS = 8
 STEPS = (
-    "w0 w1 x30 a0", "r0 z00 r1 a1", "r2 z10 a2 w2", "r3 x31 z01 Y0", "a3 r4 z11 Y1", "x20 z20 z30 Y2", "a4 w3 x32 a5", "z02 z12 Y3 x21", "a6 z21 z31 a7", "w4 x33 Y4 Y5", "x10 a8 z03 z13", "z22 z32 Y6 x22", "x11 a9 x34 Y7", "w5 x12 z04 z14", "Y8 x23 x13 z23", "z33 Y9 x24 x14", "w6 x35 x15 z05", "z15 z24 z34 x36", "x16 w7 z40 z50", "x25 z06 z16 z25", "z35 x26 x17 z41", "z51 x37 z07 z17", "z26 z36 z42 z52", "x27 f0 f1 z60", "z70 z27 z37 o0", "F0 z43 z53 o1", "F1 z61 z71 o2", "f2 f3 z80 z90", "o3 z44 z54 z62", "z72 F2 z81 z91", "F3 g010 z45 z55", "g011 g013 z63 z73", "g012 z82 z92 z46", "z56 z64 z74 z83", "z93 z47 z57 z65", "z75 z84 z94 f4", "f5 z66 z76 z85", "F4 z95 z67 F5", "z77 z86 z96 f6", "f7 z87 z97 F6", "f8 F7 f9 g230", "g231 g233 F8 g232", "F9",
+    "w0 r0 w1 r1", "r2 a0 a1 z00", "z10 r3 w2 r4", "a2 a3 z20 z30", "Y0 Y1 z01 z11", "a4 a5 z40 z50", "w3 Y2 Y3 z21", "x30 a6 a7 z31", "z02 z12 z60 z70", "Y4 z41 z51 a8", "a9 z80 z90 Y5", "x31 w4 Y6 z22", "z32 Y7 z03 z13", "z61 z71 x32 Y8", "Y9 z42 z52 z81", "z91 w5 x33 x10", "z23 z33 x20 x11", "z04 z14 z62 z72", "x12 z43 z53 x21", "x13 z82 z92 x34", "x14 w6 z24 z34", "x22 z05 z15 z63", "z73 z44 z54 x35", "x15 z83 z93 x23", "w7 z25 z35 z06", "z16 z64 z74 x24", "z45 z55 x16 z84", "z94 x36 z26 z36", "z07 z17 z65 z75", "z46 z56 x25 z85", "z95 z27 z37 x37", "f0 f1 x17 z66", "z76 F0 z47 z57", "F1 z86 z96 f2", "f3 x26 z67 z77", "F2 f4 f5 F3", "z87 z97 f6 f7", "F4 F5 f8 f9", "x27 F6 F7 o0", "o1 o2 F8 o3", "g010 g011 g012 F9", "g013 g230 g231 g233", "g232",
 )
 
 
@@ -99,6 +100,23 @@
             pl.semaphore_signal(barrier, inc=1, device_id=device, device_id_type=MESH)
     pl.semaphore_wait(barrier, len(greet) + sum(there.astype(jnp.int32) for there, _ in edges))
 
+    def w_rows(zl_from, x_from, core_from):
+        index = (zl_from * XS + x_from) * CORES + core_from
+        return w_ref.at[pl.ds(pl.multiple_of(index * depth, 16), depth)]
+
+    def w_up(zl_from, src):
+        @pl.when(has_up)
+        def _():
+            remote(src, w_rows(zl_from, x, core), wz_up.at[zl_from], wz_recv.at[zl_from], up).start()
+
+    def w_down(zl_from, src):
+        @pl.when(has_down)
+        def _():
+            remote(src, w_rows(zl_from, x, core), wz_down.at[zl_from], wz_recv.at[zl_from], down).start()
+
+    w_up(zl, w_hbm)
+    w_down(zl, w_hbm)
+
     @pl.when(has_after & jnp.logical_not(crosses))
     def _():
         for h in range(heads):
@@ -110,42 +128,32 @@
     def _():
         for h in range(heads):
             columns = pl.ds(h * HD, HD)
-            remote(k_hbm.at[:, columns], relay_ref.at[h], kv_send, relay_recv.at[h], x_peer(1)).start()
-            remote(v_hbm.at[:, columns], relay_ref.at[h], kv_send, relay_recv.at[h], up).start()
+            first = x_peer(1) if h < KEYS_BY_X else up
+            remote(k_hbm.at[:, columns], relay_ref.at[0, h], kv_send, relay_recv.at[0, h], first).start()
+            remote(v_hbm.at[:, columns], relay_ref.at[1, h], kv_send, relay_recv.at[1, h], up).start()
 
     def pass_on(h):
-        @pl.when(by_x)
-        def _():
-            landed(relay_ref.at[h], relay_recv.at[h])
-            remote(relay_ref.at[h], pk_ref.at[h], relay_send, kv_recv.at[0, h], forward).start()
+        def relay(which, device):
+            landed(relay_ref.at[which, h], relay_recv.at[which, h])
+            dst = (pk_ref, pv_ref)[which].at[h]
+            remote(relay_ref.at[which, h], dst, relay_send, kv_recv.at[which, h], device).start()
+
+        if h < KEYS_BY_X:
+            @pl.when(by_x)
+            def _():
+                relay(0, forward)
 
         @pl.when(by_z)
         def _():
-            landed(relay_ref.at[h], relay_recv.at[h])
-            remote(relay_ref.at[h], pv_ref.at[h], relay_send, kv_recv.at[1, h], back).start()
-
-    def w_rows(zl_from, x_from, core_from):
-        index = (zl_from * XS + x_from) * CORES + core_from
-        return w_ref.at[pl.ds(pl.multiple_of(index * depth, 16), depth)]
-
-    def w_up(zl_from, src):
-        @pl.when(has_up)
-        def _():
-            remote(src, w_rows(zl_from, x, core), wz_up.at[zl_from], wz_recv.at[zl_from], up).start()
-
-    def w_down(zl_from, src):
-        @pl.when(has_down)
-        def _():
-            remote(src, w_rows(zl_from, x, core), wz_down.at[zl_from], wz_recv.at[zl_from], down).start()
+            if h >= KEYS_BY_X:
+                relay(0, back)
+            relay(1, back)
 
     def w_across(zl_from, src):
         dst = w_rows(zl_from, x, core)
         for k in (1, 3):
             remote(src, dst, wx_send, wx_recv.at[k - 1, zl_from], x_peer(k)).start()
         remote(src, dst, ws_send, ws_recv, sibling).start()
-
-    w_up(zl, w_hbm)
-    w_down(zl, w_hbm)
 
     def w_both(t, work):
         @pl.when(zl >= t)
@@ -307,9 +315,14 @@
         store.start()
         stores.append(store)
 
-    @pl.when(by_x | by_z)
-    def _():
-        landed(relay_ref, relay_send)
+    @pl.when(by_x)
+    def _():
+        landed(relay_ref.at[0, pl.ds(0, KEYS_BY_X)], relay_send)
+
+    @pl.when(by_z)
+    def _():
+        landed(relay_ref.at[1], relay_send)
+        landed(relay_ref.at[0, pl.ds(KEYS_BY_X, heads - KEYS_BY_X)], relay_send)
 
     @pl.when(has_after)
     def _():
@@ -356,7 +369,7 @@
             pltpu.VMEM((tokens, width), bf16),
             pltpu.VMEM((heads, tokens, HD), bf16),
             pltpu.VMEM((heads, tokens, HD), bf16),
-            pltpu.VMEM((heads, tokens, HD), bf16),
+            pltpu.VMEM((2, heads, tokens, HD), bf16),
             pltpu.VMEM((whole, width), bf16),
             pltpu.VMEM((sources, heads, tokens, HD), bf16),
             pltpu.VMEM((pieces, HOPS - 1, ROWS, HD), bf16),
@@ -366,7 +379,7 @@
             dma,
             dma((2, heads)),
             dma,
-            dma((heads,)),
+            dma((2, heads)),
             dma((zl_count,)),
             dma((zl_count,)),
             dma((zl_count,)),

time: 123 us -> 116 us (0.943)
  the two profiles are of different devices: /device:TPU:8 before, /device:TPU:1 now
where the time goes in v3:
time: 116 us; the launch traced here: 115 us
  Pallas kernels  113 us (97%)
  local copies, waits for them, and re-layouts  1.98 us (2%)
    pallas_call x1, Pallas kernels, shards(): pl.pallas_call(functools.partial(kernel, zl_count), out_shape=jax.ShapeDt...  113 us

profile of v3, /device:TPU:1, one launch (start us, length us, event | category | flops | bytes accessed | tf_op | source)
XLA Modules:
  0.0 115.5 jit_solution(2770768723348973468)
XLA Ops:
  0.7 112.9 %shard_map.73 = bf16[512,640]{1,0:T(8,128)(2,1)} custom-call(bf16[512,640]{1,0:T(8,128)(2,1)} %res_hbm.1, bf16[512,640]{1,0:T(8,128)(2,1)} %q_hbm.1, bf16[512,640]{1,0:T(8,128)(2,1)} %k_hbm.1, bf16[512,640]{1,0:T(8,128)(2,1)} %v_hbm.1, bf16[80,640]{1,0:T(8,128)(2,1)} %w_hbm.1, f32[64,640]{1,0:T(8,128)} %gate_ref.1, s32[1]{0:T(128)S(6)} %copy.9.level_ref), custom_call_target="tpu_custom_call" | custom-call | tf_op jit(solution)/shard_map/pallas_call | solution.py:359
  113.5 2.0 %copy.10 = bf16[512,640]{1,0:T(8,128)(2,1)} copy(bf16[512,640]{1,0:T(8,128)(2,1)} %shard_map.73) | data formatting | bytes 1310720

commit v4 on v3

--- a/solution.py
+++ b/solution.py
@@ -15,16 +15,16 @@
 KEYS_BY_X = 3
 HOPS = 8
 STEPS = (
-    "w0 r0 w1 r1", "r2 a0 a1 z00", "z10 r3 w2 r4", "a2 a3 z20 z30", "Y0 Y1 z01 z11", "a4 a5 z40 z50", "w3 Y2 Y3 z21", "x30 a6 a7 z31", "z02 z12 z60 z70", "Y4 z41 z51 a8", "a9 z80 z90 Y5", "x31 w4 Y6 z22", "z32 Y7 z03 z13", "z61 z71 x32 Y8", "Y9 z42 z52 z81", "z91 w5 x33 x10", "z23 z33 x20 x11", "z04 z14 z62 z72", "x12 z43 z53 x21", "x13 z82 z92 x34", "x14 w6 z24 z34", "x22 z05 z15 z63", "z73 z44 z54 x35", "x15 z83 z93 x23", "w7 z25 z35 z06", "z16 z64 z74 x24", "z45 z55 x16 z84", "z94 x36 z26 z36", "z07 z17 z65 z75", "z46 z56 x25 z85", "z95 z27 z37 x37", "f0 f1 x17 z66", "z76 F0 z47 z57", "F1 z86 z96 f2", "f3 x26 z67 z77", "F2 f4 f5 F3", "z87 z97 f6 f7", "F4 F5 f8 f9", "x27 F6 F7 o0", "o1 o2 F8 o3", "g010 g011 g012 F9", "g013 g230 g231 g233", "g232",
+    "w0 r0 w1 r1", "r2 a0 a1 z00", "z10 r3 w2 r4", "a2 a3 z20 z30", "Y0 Y1 z01 z11", "a4 a5 z40 z50", "w3 Y2 Y3 z21", "x30 a6 a7 z31", "z02 z12 z60 z70", "Y4 z41 z51 a8", "a9 Y5 x31 w4", "Y6 z22 z32 Y7", "z03 z13 z80 z90", "z61 z71 x32 Y8", "Y9 z42 z52 w5", "z23 z33 x33 x10", "z04 z14 x20 x11", "z81 z91 z62 z72", "x12 z43 z53 x21", "x13 w6 x34 x14", "z24 z34 z05 z15", "x22 z82 z92 z63", "z73 x35 x15 z44", "z54 x23 w7 z25", "z35 z06 z16 z83", "z93 z64 z74 x36", "x16 z45 z55 z26", "z36 x24 z07 z17", "z84 z94 z65 z75", "x25 z46 z56 z27", "z37 x37 f0 f1", "x17 z85 z95 F0", "z66 z76 F1 z47", "z57 f2 f3 x26", "z86 z96 F2 z67", "z77 F3 f4 f5", "z87 z97 F4 f6", "f7 f8 f9 F5", "x27 F6 o0 F7", "o1 o2 F8 o3", "g010 g011 F9 g012", "g013 g230 g231 g233", "g232",
 )
 
 
 def kernel(
     zl_count,
     res_hbm, q_hbm, k_hbm, v_hbm, w_hbm, gate_ref, level_ref,
-    out_hbm,
-    q_ref, k_ref, v_ref, res_ref, out_ref, pk_ref, pv_ref, relay_ref, w_ref, a_ref, hop_ref, acc_ref,
-    load_sem, store_sem,
+    out_ref,
+    q_ref, k_ref, v_ref, res_ref, pk_ref, pv_ref, relay_ref, w_ref, a_ref, hop_ref, acc_ref,
+    load_sem,
     kv_send, kv_recv, relay_send, relay_recv, wz_up, wz_down, wz_recv, wx_send, wx_recv, ws_send, ws_recv,
     hop_send, hop_recv, ay_send, ay_own, ay_far,
 ):
@@ -305,15 +305,11 @@
                     project_source(numbers[0], zh, 0, heads, part, first=numbers[0] == 0)
                 else:
                     project_source(numbers[2], other, numbers[0], numbers[1] + 1, part)
-    stores = []
     for part in range(parts):
         for k in (0, 1, 3, 2):
             project_source(k, other, heads - 1, heads, part)
         rows = pl.ds(part * ROWS, ROWS)
         out_ref[rows] = (res_ref[rows].astype(jnp.float32) + gate_row * acc_ref[rows]).astype(jnp.bfloat16)
-        store = pltpu.make_async_copy(out_ref.at[rows], out_hbm.at[rows], store_sem.at[part])
-        store.start()
-        stores.append(store)
 
     @pl.when(by_x)
     def _():
@@ -341,8 +337,6 @@
     landed(w_ref.at[pl.ds(0, XS * zl_count * depth)], ws_send)
     landed(a_ref, hop_send)
     landed(a_ref.at[pl.ds(0, 6)], ay_send)
-    for store in stores:
-        store.wait()
 
 
 def shards(residual, queries, keys, values, out_weight, gate_table, levels):
@@ -360,9 +354,8 @@
         functools.partial(kernel, zl_count),
         out_shape=jax.ShapeDtypeStruct(residual.shape, bf16),
         in_specs=[anywhere] * 5 + [pl.BlockSpec(memory_space=pltpu.VMEM), pl.BlockSpec(memory_space=pltpu.SMEM)],
-        out_specs=anywhere,
+        out_specs=pl.BlockSpec(memory_space=pltpu.VMEM),
         scratch_shapes=[
-            pltpu.VMEM((tokens, width), bf16),
             pltpu.VMEM((tokens, width), bf16),
             pltpu.VMEM((tokens, width), bf16),
             pltpu.VMEM((tokens, width), bf16),
@@ -375,7 +368,6 @@
             pltpu.VMEM((pieces, HOPS - 1, ROWS, HD), bf16),
             pltpu.VMEM((tokens, width), jnp.float32),
             dma((5,)),
-            dma((tokens // ROWS,)),
             dma,
             dma((2, heads)),
             dma,

time: 116 us -> 114 us (0.983)
    pallas_call x1, Pallas kernels: 113 us -> 112 us  [shards(): pl.pallas_call(functools.partial(kernel, zl_count), out_shape=jax.ShapeDt...]
where the time goes in v4:
time: 114 us
  Pallas kernels  112 us (98%)
  local copies, waits for them, and re-layouts  1.98 us (2%)
    pallas_call x1, Pallas kernels, shards(): pl.pallas_call(functools.partial(kernel, zl_count), out_shape=jax.ShapeDt...  112 us

profile of v4, /device:TPU:1, one launch (start us, length us, event | category | flops | bytes accessed | tf_op | source)
XLA Modules:
  0.0 114.3 jit_solution(3774822982216415338)
XLA Ops:
  0.7 111.6 %shard_map.73 = bf16[512,640]{1,0:T(8,128)(2,1)} custom-call(bf16[512,640]{1,0:T(8,128)(2,1)} %res_hbm.1, bf16[512,640]{1,0:T(8,128)(2,1)} %q_hbm.1, bf16[512,640]{1,0:T(8,128)(2,1)} %k_hbm.1, bf16[512,640]{1,0:T(8,128)(2,1)} %v_hbm.1, bf16[80,640]{1,0:T(8,128)(2,1)} %w_hbm.1, f32[64,640]{1,0:T(8,128)} %gate_ref.1, s32[1]{0:T(128)S(6)} %copy.9.level_ref), custom_call_target="tpu_custom_call" | custom-call | tf_op jit(solution)/shard_map/pallas_call | solution.py:353
  112.3 2.0 %copy.10 = bf16[512,640]{1,0:T(8,128)(2,1)} copy(bf16[512,640]{1,0:T(8,128)(2,1)} %shard_map.73) | data formatting | bytes 1310720

commit v5 on v4

--- a/solution.py
+++ b/solution.py
@@ -87,7 +87,7 @@
     own_w.start()
 
     barrier = pltpu.get_barrier_semaphore()
-    greet = [sibling, ring_peer(1)[0], ring_peer(-1)[0]] + [x_peer(k) for k in (1, 3)] + [y_peer(k) for k in (1, 3)]
+    greet = [sibling, ring_peer(1)[0], ring_peer(-1)[0]] + [x_peer(k) for k in (1, 3)] + [y_peer(k) for k in (1, 2, 3)]
     for device in greet:
         pl.semaphore_signal(barrier, inc=1, device_id=device, device_id_type=MESH)
     edges = (
@@ -214,7 +214,8 @@
         remote(src, dst, hop_send, hop_recv.at[p, hop], device).start()
 
     def y_send(source, p, arrived):
-        for k in (1, 3):
+        direct = arrived is ay_far and p >= pieces - parts
+        for k in (2, 1, 3) if direct else (1, 3):
             remote(piece(source, p), piece(source, p), ay_send, arrived.at[k - 1, p], y_peer(k)).start()
 
     scale = math.log2(math.e) / math.sqrt(HD)
@@ -264,6 +265,8 @@
             landed(piece(source_of(k, side), p), (ay_own if side is zh else ay_far).at[k - 1, p])
 
     def y_pass(side, p):
+        if side is not zh and p >= pieces - parts:
+            return
         k = 1 if p % 2 == 0 else 3
         y_landed(k, side, p)
         ref = piece(source_of(k, side), p)

time: 114 us -> 115 us (level)
  no operation moved by 1% of the time
where the time goes in v5:
time: 115 us
  Pallas kernels  113 us (98%)
  local copies, waits for them, and re-layouts  1.98 us (2%)
    pallas_call x1, Pallas kernels, shards(): pl.pallas_call(functools.partial(kernel, zl_count), out_shape=jax.ShapeDt...  113 us

profile of v5, /device:TPU:1, one launch (start us, length us, event | category | flops | bytes accessed | tf_op | source)
XLA Modules:
  0.0 115.2 jit_solution(17794302019942018159)
XLA Ops:
  0.7 112.5 %shard_map.73 = bf16[512,640]{1,0:T(8,128)(2,1)} custom-call(bf16[512,640]{1,0:T(8,128)(2,1)} %res_hbm.1, bf16[512,640]{1,0:T(8,128)(2,1)} %q_hbm.1, bf16[512,640]{1,0:T(8,128)(2,1)} %k_hbm.1, bf16[512,640]{1,0:T(8,128)(2,1)} %v_hbm.1, bf16[80,640]{1,0:T(8,128)(2,1)} %w_hbm.1, f32[64,640]{1,0:T(8,128)} %gate_ref.1, s32[1]{0:T(128)S(6)} %copy.9.level_ref), custom_call_target="tpu_custom_call" | custom-call | tf_op jit(solution)/shard_map/pallas_call | solution.py:356
  113.2 2.0 %copy.10 = bf16[512,640]{1,0:T(8,128)(2,1)} copy(bf16[512,640]{1,0:T(8,128)(2,1)} %shard_map.73) | data formatting | bytes 1310720
